TPU v7x, 32 devices: a whole 2x2x4 slice. The times are simulated.
32 devices in a mesh: frag: 2 (over x), pair: 16 (over z, y, core).
Axes of the slice: x: 2, y: 2, z: 4, core: 2. Of those that a mesh axis runs over, the one named last changes fastest.
Arguments:
- amplitudes: bfloat16 [64, 640, 640], P(('frag', 'pair')), parts along dimension 0, may hold values from -6 to 6
- pair_ints: bfloat16 [64, 640, 640], P(('frag', 'pair')), parts along dimension 0, may hold values from -6 to 6
- int_tiles: bfloat16 [128, 128, 128], P(('frag', 'pair')), parts along dimension 0, may hold values from -0.25 to 0.25
- tile_owner: int32 [4000, 1], P('frag'), parts along dimension 0, may hold values from 0 to 15; in each aligned block of 125 rows (0 to 124, 125 to 249, ...) at most 16 rows name the same one
- tile_slot: int32 [4000], P('frag'), parts along dimension 0, may hold values from 0 to 3
- tile_extent: int32 [32, 5], P(('frag', 'pair')), parts along dimension 0, may hold values from 64 to 128, as said below
- tile_mask: int32 [64, 5, 5], P(('frag', 'pair')), parts along dimension 0, may hold values 0 or 1
- mirror_slot: int32 [64], P(('frag', 'pair')), parts along dimension 0, may hold values from 0 to 1, as said below
Outputs:
- residual: float32 [64, 640, 640], P(('frag', 'pair')), parts along dimension 0
There are 2 independent parts, one for each index of `frag`. A program takes and returns all parts, laid end to end along the dimension named above; each array names one. Nothing has to cross between parts.
Inputs may be any that keep to these rules, and one draw needn't show every extreme that they name: `tile_owner`: in each aligned block of 125 rows (the tiles read by one pair block) no owner is named by more than 16 rows, a bound that some block reaches. `tile_extent`: row d and row (d + 8) % 16 are equal: a pair block and its mirror share one domain. `mirror_slot`: for each pair block, its 2 entries are a permutation of 0 to 1, and the entries of the mirror block are the inverse permutation.
All inputs are finite; a program needn't handle non-finite values. No bound on the sum of `tile_mask` on one device may be relied on, other than what follows from the above.
Results may differ from a plain program's by a relative error of at most 0.002.
Values may be sent and summed in bfloat16 or wider, within the bound.
A program may use at most 128 MiB of HBM per device.

v0:
```python
import jax
import jax.numpy as jnp
from jax import lax
from jax.sharding import PartitionSpec as P

VT = 128
KDOM = 5
NAUXW = 4
DOM = 640
NEED_DEV = 125


def passed_along(value, axis, steps):
    count = lax.axis_size(axis)
    pairs = [(source, (source + steps) % count) for source in range(count)]
    return lax.ppermute(value, axis, pairs)


def domain_mask(tile_flags, extent_row):
    position = jnp.arange(KDOM * VT)
    live_rows = (position % VT < extent_row[position // VT]).astype(jnp.float32)
    full_flags = jnp.repeat(jnp.repeat(tile_flags.astype(jnp.float32), VT, axis=1), VT, axis=2)
    return (full_flags * live_rows[None, :, None] * live_rows[None, None, :]).astype(jnp.bfloat16)


def shards(
    amplitudes, pair_ints, int_tiles, tile_owner, tile_slot, tile_extent, tile_mask, mirror_slot
):
    devices = lax.axis_size("pair")
    own_index = lax.axis_index("pair")
    slot_count = max(2, (2 * NEED_DEV + devices - 1) // devices)
    owners = tile_owner[:, 0].reshape(devices, NEED_DEV)
    places = tile_slot.reshape(devices, NEED_DEV)
    own_owner = lax.dynamic_index_in_dim(owners, own_index, 0, keepdims=False)
    mine = (owners == own_index).astype(jnp.int32)
    rank_mine = jnp.cumsum(mine, axis=1) - mine
    slot_ids = jnp.arange(slot_count)
    chosen = (mine[:, None, :] == 1) & (rank_mine[:, None, :] == slot_ids[None, :, None])
    filled = jnp.any(chosen, axis=2)
    local_index = jnp.sum(jnp.where(chosen, places[:, None, :], 0), axis=2)
    taken = jnp.take(int_tiles, local_index, axis=0)
    outgoing = jnp.where(filled[:, :, None, None], taken, jnp.zeros_like(taken))
    incoming = lax.all_to_all(outgoing, "pair", split_axis=0, concat_axis=0, tiled=True)
    need_ids = jnp.arange(NEED_DEV)
    same_owner = own_owner[:, None] == own_owner[None, :]
    earlier = need_ids[None, :] < need_ids[:, None]
    rank_own = jnp.sum((same_owner & earlier).astype(jnp.int32), axis=1)
    flat_slot = own_owner * slot_count + rank_own
    op_tiles = jnp.take(incoming.reshape(devices * slot_count, VT, VT), flat_slot, axis=0)
    operators = (
        op_tiles.reshape(1 + NAUXW, KDOM, KDOM, VT, VT)
        .transpose(0, 1, 3, 2, 4)
        .reshape(1 + NAUXW, DOM, DOM)
    )
    fock_op = operators[0]
    factors = operators[1:]
    dmask = domain_mask(tile_mask, tile_extent[0])
    masked = amplitudes * dmask
    fock_term = jnp.einsum(
        "ac,qcb->qab", fock_op, masked, preferred_element_type=jnp.float32
    ) + jnp.einsum("qac,bc->qab", masked, fock_op, preferred_element_type=jnp.float32)
    local_part = pair_ints.astype(jnp.float32) + fock_term
    shift_by = devices // 2
    half_ladder = jnp.einsum(
        "pac,qcd->qpad", factors, masked, preferred_element_type=jnp.float32
    ).astype(jnp.bfloat16)
    ladder = jnp.einsum("qpad,pbd->qab", half_ladder, factors, preferred_element_type=jnp.float32)
    local_res = local_part + ladder
    partner = passed_along(local_res, "pair", shift_by)
    mirror = jnp.swapaxes(jnp.take(partner, mirror_slot, axis=0), 1, 2)
    return dmask.astype(jnp.float32) * (local_res + mirror)


def solution(mesh):
    in_specs = (
        P(("frag", "pair"), None, None),
        P(("frag", "pair"), None, None),
        P(("frag", "pair"), None, None),
        P("frag", None),
        P("frag"),
        P(("frag", "pair"), None),
        P(("frag", "pair"), None, None),
        P(("frag", "pair")),
    )
    out_specs = P(("frag", "pair"), None, None)
    return jax.shard_map(shards, mesh=mesh, in_specs=in_specs, out_specs=out_specs, check_vma=False)
```

profile of v0, /device:TPU:0, one launch (start us, length us, event | category | flops | bytes accessed | tf_op | source)
XLA Modules:
  0.0 416.5 jit_solution(12176107937155911936)
XLA Ops:
  0.5 1.4 reduce.9
  2.3 0.8 broadcast_in_dim.78
  3.9 8.3 %gather_fusion = bf16[256,128,128]{2,1,0:T(8,128)(2,1)} fusion(bf16[4,128,128]{2,1,0:T(8,128)(2,1)S(1)} %copy-done, s32[1024]{0:T(1024)S(1)} %pad_clamp_fusion.2), kind=kCustom, calls=%fused_computation | custom fusion | bytes 16778240 | tf_op jit(solution)/shard_map/jit(_take)/gather | solution.py:41
  12.2 7.4 %select_select_fusion = bf16[16,16,128,128]{3,2,1,0:T(8,128)(2,1)} fusion(bf16[16,16,128,128]{3,2,1,0:T(8,128)(2,1)} %bitcast.66, pred[16,16]{1,0:T(8,128)(4,1)S(1)} %compare_and_fusion.1, pred[16,16]{1,0:T(8,128)(4,1)S(1)} %fusion.15), kind=kLoop, calls=%fused_computation.3 | loop fusion | flops 8388608 | bytes 16777728 | tf_op jit(solution)/shard_map/jit(_where)/select_n | solution.py:42
  19.6 7.6 %all-to-all-start = ((bf16[16,16,128,128]{3,2,1,0:T(8,128)(2,1)}), bf16[16,16,128,128]{3,2,1,0:T(8,128)(2,1)}, u32[]{:S(2)}, u32[]{:S(2)}) async-start(bf16[16,16,128,128]{3,2,1,0:T(8,128)(2,1)} %select_select_fusion), calls=%async_computation | async-start | bytes 16777216 | tf_op jit(solution)/shard_map/all_to_all | solution.py:43
  27.9 1.4 copy.30
  29.3 3.5 copy.29
  33.5 3.2 fusion.22
  37.2 140.7 %all-to-all-done = bf16[16,16,128,128]{3,2,1,0:T(8,128)(2,1)} async-done(((bf16[16,16,128,128]{3,2,1,0:T(8,128)(2,1)}), bf16[16,16,128,128]{3,2,1,0:T(8,128)(2,1)}, u32[]{:S(2)}, u32[]{:S(2)}) %all-to-all-start) | async-done | bytes 8388640 | tf_op jit(solution)/shard_map/all_to_all | solution.py:43
  178.0 6.4 %gather_fusion.1 = bf16[125,128,128]{2,1,0:T(8,128)(2,1)} fusion(bf16[256,128,128]{2,1,0:T(8,128)(2,1)} %bitcast.9, s32[1024]{0:T(1024)S(1)} %pad_clamp_fusion.1), kind=kCustom, calls=%fused_computation.1 | custom fusion | bytes 8192500 | tf_op jit(solution)/shard_map/jit(_take)/gather | solution.py:49
  184.4 2.6 select_bitcast_fusion
  187.0 1.9 copy-done.2
  189.5 1.8 reshape.246
  191.3 4.5 %fusion.26 = f32[2,640,640]{2,1,0:T(8,128)} fusion(bf16[2,640,640]{1,2,0:T(8,128)(2,1)S(1)} %fusion.7, bf16[640,640,1]{1,0,2:T(8,128)(2,1)} %reshape.246), kind=kOutput, calls=%fused_computation.62 | convolution fusion | flops 1048576000 | bytes 5734400 | tf_op jit(solution)/shard_map/ac,qcb->qab/dot_general | solution.py:59
  195.9 3.2 fusion.27
  199.0 5.1 %copy.34 = bf16[4,5,128,5,128]{4,3,2,1,0:T(8,128)(2,1)} copy(bf16[4,5,128,5,128]{4,2,3,1,0:T(8,128)(2,1)S(1)} %slice-done) | data formatting | bytes 6553600 | tf_op jit(solution)/shard_map/slice | solution.py:56
  204.2 8.3 %reshape.248 = bf16[4,640,640,1]{2,1,0,3:T(8,128)(2,1)} reshape(bf16[4,5,128,5,128]{4,3,2,1,0:T(8,128)(2,1)} %copy.34) | data formatting | bytes 6553600 | tf_op jit(solution)/shard_map/slice | solution.py:56
  212.5 16.6 %bitcast_add_fusion.1 = f32[2,640,640]{1,2,0:T(8,128)S(1)} fusion(f32[2,640,640]{1,2,0:T(8,128)} %fusion.27, f32[2,640,640]{2,1,0:T(8,128)} %fusion.26, bf16[2,640,640]{1,2,0:T(8,128)(2,1)} %copy.29, bf16[4,640,640,1]{2,1,0,3:T(8,128)(2,1)} %reshape.248, bf16[2,640,640]{1,2,0:T(8,128)(2,1)} %copy-done.5), kind=kOutput, calls=%fused_computation.10 | convolution fusion | flops 8395161600 | bytes 16384000 | tf_op jit(solution)/shard_map/qpad,pbd->qab/dot_general | solution.py:67
  229.1 34.7 %collective-permute-start = (f32[2,640,640]{1,2,0:T(8,128)S(1)}, f32[2,640,640]{1,2,0:T(8,128)}, u32[]{:S(2)}, u32[]{:S(2)}) collective-permute-start(f32[2,640,640]{1,2,0:T(8,128)S(1)} %bitcast_add_fusion.1), channel_id=1, source_target_pairs={{0,8},{1,9},{2,10},{3,11},{4,12},{5,13},{6,14},{7,15},{8,0},{9,1},... | collective-permute-start | bytes 9830408 | tf_op jit(solution)/shard_map/ppermute | solution.py:16
  263.9 140.3 %collective-permute-done = f32[2,640,640]{1,2,0:T(8,128)} collective-permute-done((f32[2,640,640]{1,2,0:T(8,128)S(1)}, f32[2,640,640]{1,2,0:T(8,128)}, u32[]{:S(2)}, u32[]{:S(2)}) %collective-permute-start) | collective-permute-done | bytes 3276832 | tf_op jit(solution)/shard_map/ppermute | solution.py:16
  404.2 3.4 copy.37
  407.6 2.4 gather_fusion.2
  410.0 3.5 fusion.3
  413.5 3.0 copy.38
  (52 shorter events, 4.2 us)
Async XLA Ops:
  0.0 3.9 copy-start
  19.6 8.1 %copy-start.8 = (s32[2,5,5]{2,0,1:T(2,128)S(1)}, s32[2,5,5]{2,0,1:T(2,128)}, u32[]{:S(2)}) copy-start(s32[2,5,5]{2,0,1:T(2,128)} %param.14) | copy-start | bytes 604
  19.6 8.3 %copy-start.4 = (bf16[2,640,640]{2,1,0:T(8,128)(2,1)S(1)}, bf16[2,640,640]{2,1,0:T(8,128)(2,1)}, u32[]{:S(2)}) copy-start(bf16[2,640,640]{2,1,0:T(8,128)(2,1)} %param.8) | copy-start | bytes 4915204
  19.6 158.4 %all-to-all-start = ((bf16[16,16,128,128]{3,2,1,0:T(8,128)(2,1)}), bf16[16,16,128,128]{3,2,1,0:T(8,128)(2,1)}, u32[]{:S(2)}, u32[]{:S(2)}) async-start(bf16[16,16,128,128]{3,2,1,0:T(8,128)(2,1)} %select_select_fusion), calls=%async_computation | async-start | bytes 16777216 | tf_op jit(solution)/shard_map/all_to_all | solution.py:43
  27.9 4.9 %copy-start.7 = (s32[1,5]{1,0:T(1,128)S(1)}, s32[1,5]{1,0:T(1,128)}, u32[]{:S(2)}) copy-start(s32[1,5]{1,0:T(1,128)} %param.13) | copy-start | bytes 64
  37.1 158.7 %copy-start.5 = (bf16[2,640,640]{1,2,0:T(8,128)(2,1)}, bf16[2,640,640]{1,2,0:T(8,128)(2,1)S(1)}, u32[]{:S(2)}) copy-start(bf16[2,640,640]{1,2,0:T(8,128)(2,1)S(1)} %fusion.7) | copy-start | bytes 4915204
  187.0 1.9 copy-start.2
  191.3 4.6 %copy-start.6 = (bf16[640,640,1]{1,0,2:T(8,128)(2,1)S(1)}, bf16[640,640,1]{1,0,2:T(8,128)(2,1)}, u32[]{:S(2)}) copy-start(bf16[640,640,1]{1,0,2:T(8,128)(2,1)} %reshape.246) | copy-start | bytes 2457604
  195.9 3.2 slice-start
  212.5 51.4 %copy-start.9 = (s32[2]{0:T(128)S(1)}, s32[2]{0:T(128)}, u32[]{:S(2)}) copy-start(s32[2]{0:T(128)} %param.15) | copy-start | bytes 28
  229.1 34.8 %copy-start.3 = (f32[2,640,640]{1,2,0:T(8,128)}, f32[2,640,640]{1,2,0:T(8,128)S(1)}, u32[]{:S(2)}) copy-start(f32[2,640,640]{1,2,0:T(8,128)S(1)} %bitcast_add_fusion.1) | copy-start | bytes 9830404
  229.1 175.1 %collective-permute-start = (f32[2,640,640]{1,2,0:T(8,128)S(1)}, f32[2,640,640]{1,2,0:T(8,128)}, u32[]{:S(2)}, u32[]{:S(2)}) collective-permute-start(f32[2,640,640]{1,2,0:T(8,128)S(1)} %bitcast_add_fusion.1), channel_id=1, source_target_pairs={{0,8},{1,9},{2,10},{3,11},{4,12},{5,13},{6,14},{7,15},{8,0},{9,1},... | collective-permute-start | bytes 9830408 | tf_op jit(solution)/shard_map/ppermute | solution.py:16
  410.0 6.4 %copy-start.1 = (bf16[4,128,128]{2,1,0:T(8,128)(2,1)S(1)}, bf16[4,128,128]{2,1,0:T(8,128)(2,1)}, u32[]{:S(2)}) copy-start(bf16[4,128,128]{2,1,0:T(8,128)(2,1)} %param.10) | copy-start | bytes 393220
where the time goes:
time: 417 us; the launch traced here: 416 us
  waiting for transfers between devices  281 us (67%)
  local copies, waits for them, and re-layouts  48.7 us (12%)
  starting transfers between devices  42.4 us (10%)
  matrix products  24.3 us (6%)
  other arithmetic  19.7 us (5%)
    all_to_all x1, waiting for transfers between devices, shards(): lax.all_to_all(outgoing, 'pair', split_axis=0, concat_axis=0, tiled=True)  141 us
    ppermute x1, waiting for transfers between devices, passed_along(): return lax.ppermute(value, axis, pairs)  140 us
    ppermute x1, starting transfers between devices, passed_along(): return lax.ppermute(value, axis, pairs)  34.7 us
    dot_general x1, matrix products, shards(): jnp.einsum('qpad,pbd->qab', half_ladder, factors, preferred_element_type=...  16.6 us
    slice x4, local copies, waits for them, and re-layouts, shards(): factors = operators[1:]  13.4 us
  transfers between devices with their start and end apart: 2, of which 2 were waited for; matrix products, arithmetic and copies ran while one was open for 2% of the time, Pallas kernels for 0%

commit v1 on v0

--- a/solution.py
+++ b/solution.py
@@ -28,25 +28,10 @@
 ):
     devices = lax.axis_size("pair")
     own_index = lax.axis_index("pair")
-    slot_count = max(2, (2 * NEED_DEV + devices - 1) // devices)
-    owners = tile_owner[:, 0].reshape(devices, NEED_DEV)
-    places = tile_slot.reshape(devices, NEED_DEV)
-    own_owner = lax.dynamic_index_in_dim(owners, own_index, 0, keepdims=False)
-    mine = (owners == own_index).astype(jnp.int32)
-    rank_mine = jnp.cumsum(mine, axis=1) - mine
-    slot_ids = jnp.arange(slot_count)
-    chosen = (mine[:, None, :] == 1) & (rank_mine[:, None, :] == slot_ids[None, :, None])
-    filled = jnp.any(chosen, axis=2)
-    local_index = jnp.sum(jnp.where(chosen, places[:, None, :], 0), axis=2)
-    taken = jnp.take(int_tiles, local_index, axis=0)
-    outgoing = jnp.where(filled[:, :, None, None], taken, jnp.zeros_like(taken))
-    incoming = lax.all_to_all(outgoing, "pair", split_axis=0, concat_axis=0, tiled=True)
-    need_ids = jnp.arange(NEED_DEV)
-    same_owner = own_owner[:, None] == own_owner[None, :]
-    earlier = need_ids[None, :] < need_ids[:, None]
-    rank_own = jnp.sum((same_owner & earlier).astype(jnp.int32), axis=1)
-    flat_slot = own_owner * slot_count + rank_own
-    op_tiles = jnp.take(incoming.reshape(devices * slot_count, VT, VT), flat_slot, axis=0)
+    ids = (tile_owner[:, 0] * int_tiles.shape[0] + tile_slot).reshape(devices, NEED_DEV)
+    own_ids = lax.dynamic_index_in_dim(ids, own_index, 0, keepdims=False)
+    stored = lax.all_gather(int_tiles, "pair", axis=0, tiled=True)
+    op_tiles = jnp.take(stored, own_ids, axis=0)
     operators = (
         op_tiles.reshape(1 + NAUXW, KDOM, KDOM, VT, VT)
         .transpose(0, 1, 3, 2, 4)
@@ -66,8 +51,10 @@
     ).astype(jnp.bfloat16)
     ladder = jnp.einsum("qpad,pbd->qab", half_ladder, factors, preferred_element_type=jnp.float32)
     local_res = local_part + ladder
-    partner = passed_along(local_res, "pair", shift_by)
-    mirror = jnp.swapaxes(jnp.take(partner, mirror_slot, axis=0), 1, 2)
+    partner = jnp.stack(
+        [passed_along(local_res[q].astype(jnp.bfloat16), "pair", shift_by) for q in range(2)]
+    )
+    mirror = jnp.swapaxes(jnp.take(partner, mirror_slot, axis=0), 1, 2).astype(jnp.float32)
     return dmask.astype(jnp.float32) * (local_res + mirror)
 
 

time: 417 us -> 190 us (0.46)
  waiting for transfers between devices: 281 us -> 107 us
  starting transfers between devices: 42.4 us -> 2.99 us
  local copies, waits for them, and re-layouts: 48.7 us -> 30.6 us
  between operations: 0.29 us -> 13.6 us
  other arithmetic: 19.7 us -> 13.4 us
    all_to_all x1 -> x0, waiting for transfers between devices: 141 us -> none  [shards(): lax.all_to_all(outgoing, 'pair', split_axis=0, concat_axis=0, tiled=True)]
    ppermute x1 -> x2, waiting for transfers between devices: 140 us -> 71 us  [passed_along(): return lax.ppermute(value, axis, pairs)]
    all_gather x0 -> x1, waiting for transfers between devices: none -> 35.1 us  [shards(): stored = lax.all_gather(int_tiles, 'pair', axis=0, tiled=True)]
    ppermute x1 -> x2, starting transfers between devices: 34.7 us -> 2.99 us  [passed_along(): return lax.ppermute(value, axis, pairs)]
    gather x3 -> x2, local copies, waits for them, and re-layouts: 17.2 us -> 6.51 us  [the longest x1 4.58 us: shards(): op_tiles = jnp.take(stored, own_ids, axis=0)]
    all_to_all x1 -> x0, starting transfers between devices: 7.65 us -> none  [shards(): lax.all_to_all(outgoing, 'pair', split_axis=0, concat_axis=0, tiled=True)]
    select_n x4 -> x2, other arithmetic: 7.41 us -> 0.02 us  [the longest x1 0.01 us: shards(): op_tiles = jnp.take(stored, own_ids, axis=0)]
    slice x4 -> x2, local copies, waits for them, and re-layouts: 13.4 us -> 10.2 us  [shards(): factors = operators[1:]]
  transfers between devices with their start and end apart: 2 -> 3, of which waited for: 2 -> 3; matrix products, arithmetic and copies ran while one was open for 2% -> 6% of each run, Pallas kernels for 0% -> 0%
where the time goes in v1:
time: 190 us
  waiting for transfers between devices  107 us (56%)
  local copies, waits for them, and re-layouts  30.6 us (16%)
  matrix products  22.4 us (12%)
  between operations  13.6 us (7%)
  other arithmetic  13.4 us (7%)
  starting transfers between devices  2.99 us (2%)
    ppermute x2, waiting for transfers between devices, passed_along(): return lax.ppermute(value, axis, pairs)  71 us
    all_gather x1, waiting for transfers between devices, shards(): stored = lax.all_gather(int_tiles, 'pair', axis=0, tiled=True)  35.1 us
    dot_general x1, matrix products, shards(): jnp.einsum('qpad,pbd->qab', half_ladder, factors, preferred_element_type=...  14.7 us
    slice x2, local copies, waits for them, and re-layouts, shards(): factors = operators[1:]  10.2 us
    transpose x1, other arithmetic, shards(): operators = op_tiles.reshape(1 + NAUXW, KDOM, KDOM, VT, VT).transpose(0,...  5.11 us
    unnamed x14, local copies, waits for them, and re-layouts  5.06 us
    gather x1, local copies, waits for them, and re-layouts, shards(): op_tiles = jnp.take(stored, own_ids, axis=0)  4.58 us
    dot_general x1, matrix products, shards(): jnp.einsum('qac,bc->qab', masked, fock_op, preferred_element_type=jnp.flo...  4.37 us
  transfers between devices with their start and end apart: 3, of which 3 were waited for; matrix products, arithmetic and copies ran while one was open for 6% of the time, Pallas kernels for 0%

profile of v1, /device:TPU:0, one launch (start us, length us, event | category | flops | bytes accessed | tf_op | source)
XLA Modules:
  0.0 189.7 jit_solution(2897431899729012508)
XLA Ops:
  6.5 0.7 all-gather.2.cloned.1.call-update
  7.3 0.7 broadcast_multiply_fusion
  8.0 0.7 add.83
  8.9 2.8 %copy.30 = bf16[2,640,640]{1,2,0:T(8,128)(2,1)S(1)} copy(bf16[2,640,640]{2,1,0:T(8,128)(2,1)} %param.8) | data formatting | bytes 3276800 | tf_op args[0]
  12.0 2.2 %copy.29 = bf16[2,640,640]{1,2,0:T(8,128)(2,1)} copy(bf16[2,640,640]{2,1,0:T(8,128)(2,1)S(1)} %copy-done) | data formatting | bytes 3276800 | tf_op args[1]
  14.9 3.2 %fusion.20 = s32[640]{0:T(1024)S(1)} fusion(s32[]{:T(128)} %bitcast.1, s32[]{:T(128)} %bitcast.2, s32[]{:T(128)} %bitcast.3, s32[]{:T(128)} %bitcast.5, s32[]{:T(128)} %bitcast.4), kind=kLoop, calls=%fused_computation.44 | loop fusion | flops 12160 | bytes 2580 | tf_op jit(solution)/shard_map/gather | solution.py:21
  18.6 35.1 %all-gather.2.cloned.1.call-done = bf16[64,128,128]{2,1,0:T(8,128)(2,1)} async-done(((bf16[4,128,128]{2,1,0:T(8,128)(2,1)}), bf16[64,128,128]{2,1,0:T(8,128)(2,1)}) %all-gather.2.cloned.1.call-update) | async-done | bytes 2097168 | tf_op jit(solution)/shard_map/all_gather | solution.py:33
  53.7 4.6 %gather_fusion = bf16[125,128,128]{2,1,0:T(8,128)(2,1)} fusion(bf16[64,128,128]{2,1,0:T(8,128)(2,1)} %all-gather.2.cloned.1.call-done, s32[1024]{0:T(1024)S(1)} %pad_clamp_fusion.1), kind=kCustom, calls=%fused_computation | custom fusion | bytes 8192500 | tf_op jit(solution)/shard_map/jit(_take)/gather | solution.py:34
  58.2 5.1 %fusion.2 = bf16[5,5,128,5,128]{4,3,2,1,0:T(8,128)(2,1)S(1)} fusion(bf16[5,5,5,128,128]{4,3,2,1,0:T(8,128)(2,1)} %bitcast.64, pred[5,5,5]{2,1,0:T(8,128)(4,1)S(1)} %compare_and_fusion), kind=kLoop, calls=%fused_computation.5 | loop fusion | flops 2048000 | bytes 8192125 | tf_op jit(solution)/shard_map/transpose | solution.py:37
  63.3 3.2 %slice.40 = bf16[4,5,128,5,128]{4,3,2,1,0:T(8,128)(2,1)} slice(bf16[5,5,128,5,128]{4,3,2,1,0:T(8,128)(2,1)S(1)} %fusion.2), slice={[1:5], [0:5], [0:128], [0:5], [0:128]} | slice | bytes 6553600 | tf_op jit(solution)/shard_map/slice | solution.py:41
  66.8 1.8 reshape.192
  68.5 4.4 %fusion.28 = f32[2,640,640]{1,2,0:T(8,128)} fusion(bf16[640,640,1]{1,0,2:T(8,128)(2,1)} %reshape.192, bf16[2,640,640]{1,2,0:T(8,128)(2,1)S(1)} %fusion.8), kind=kOutput, calls=%fused_computation.52 | convolution fusion | flops 1048576000 | bytes 5734400 | tf_op jit(solution)/shard_map/qac,bc->qab/dot_general | solution.py:46
  72.9 3.3 %fusion.27 = f32[2,640,640]{2,1,0:T(8,128)} fusion(bf16[2,640,640]{1,2,0:T(8,128)(2,1)S(1)} %fusion.8, bf16[640,640,1]{1,0,2:T(8,128)(2,1)S(1)} %copy-done.2), kind=kOutput, calls=%fused_computation.51 | convolution fusion | flops 1048576000 | bytes 5734400 | tf_op jit(solution)/shard_map/ac,qcb->qab/dot_general | solution.py:44
  76.2 7.0 %reshape.194 = bf16[4,640,640,1]{2,1,0,3:T(8,128)(2,1)S(1)} reshape(bf16[4,5,128,5,128]{4,3,2,1,0:T(8,128)(2,1)} %slice.40) | data formatting | bytes 6553600 | tf_op jit(solution)/shard_map/slice | solution.py:41
  83.2 14.7 %fusion.24 = (bf16[2,640,640]{1,2,0:T(8,128)(2,1)}, f32[2,640,640]{1,2,0:T(8,128)}) fusion(bf16[4,640,640,1]{2,1,0,3:T(8,128)(2,1)S(1)} %reshape.194, bf16[2,640,640]{1,2,0:T(8,128)(2,1)} %copy-done.1, f32[2,640,640]{1,2,0:T(8,128)} %fusion.28, f32[2,640,640]{2,1,0:T(8,128)} %fusion.27, bf16[2,640,640]{1,2,0:T(8,128)(2,1)} %copy.29), kind=kOutput, calls=%fused_computation.50 | convolution fusion | flops 8395980800 | bytes 18022400 | tf_op jit(solution)/shard_map/qpad,pbd->qab/dot_general | solution.py:52
  97.9 1.5 slice_bitcast_fusion.1
  99.4 0.7 collective-permute-start.1
  100.2 2.3 %collective-permute-start = (bf16[640,640]{0,1:T(8,128)(2,1)S(1)}, bf16[640,640]{0,1:T(8,128)(2,1)S(1)}, u32[]{:S(2)}, u32[]{:S(2)}) collective-permute-start(bf16[640,640]{0,1:T(8,128)(2,1)S(1)} %get-tuple-element.5), channel_id=1, source_target_pairs={{0,8},{1,9},{2,10},{3,11},{4,12},{5,13},{6,14},{7,15},{8,0},{9,1},... | collective-permute-start | bytes 2457608 | tf_op jit(solution)/shard_map/ppermute | solution.py:16
  102.5 53.5 %collective-permute-done.1 = bf16[640,640]{0,1:T(8,128)(2,1)S(1)} collective-permute-done((bf16[640,640]{0,1:T(8,128)(2,1)S(1)}, bf16[640,640]{0,1:T(8,128)(2,1)S(1)}, u32[]{:S(2)}, u32[]{:S(2)}) %collective-permute-start.1) | collective-permute-done | bytes 819232 | tf_op jit(solution)/shard_map/ppermute | solution.py:16
  155.9 17.5 %collective-permute-done = bf16[640,640]{0,1:T(8,128)(2,1)S(1)} collective-permute-done((bf16[640,640]{0,1:T(8,128)(2,1)S(1)}, bf16[640,640]{0,1:T(8,128)(2,1)S(1)}, u32[]{:S(2)}, u32[]{:S(2)}) %collective-permute-start) | collective-permute-done | bytes 819232 | tf_op jit(solution)/shard_map/ppermute | solution.py:16
  173.6 1.4 copy.36
  175.0 1.9 %gather_fusion.1 = bf16[2,640,640]{2,1,0:T(8,128)(2,1)} fusion(bf16[2,640,640]{2,1,0:T(8,128)(2,1)S(1)} %copy.36, s32[1024]{0:T(1024)S(1)} %pad_clamp_fusion), kind=kCustom, calls=%fused_computation.1 | custom fusion | bytes 3276808 | tf_op jit(solution)/shard_map/jit(_take)/gather | solution.py:57
  176.9 3.0 %fusion.4 = f32[2,640,640]{1,2,0:T(8,128)S(1)} fusion(f32[2,640,640]{1,2,0:T(8,128)} %get-tuple-element.13, bf16[2,640,640]{2,1,0:T(8,128)(2,1)} %gather_fusion.1, f32[640]{0:T(1024)S(1)} %fusion.19, f32[2,640,5]{1,2,0:T(8,128)S(1)} %copy.28, pred[2]{0:T(512)(128)(4,1)S(1)} %compare_and_fusion.1), kind=kLoop, calls=%fused_computation.8 | loop fusion | flops 6553600 | bytes 8220162 | tf_op jit(solution)/shard_map/mul | solution.py:58
  179.9 3.0 %copy.37 = f32[2,640,640]{2,1,0:T(8,128)} copy(f32[2,640,640]{1,2,0:T(8,128)S(1)} %fusion.4) | data formatting | bytes 6553600 | tf_op jit(solution)/shard_map/mul | solution.py:58
  (32 shorter events, 2.0 us)
Async XLA Ops:
  6.5 5.2 %copy-start.4 = (s32[2,5,5]{2,0,1:T(2,128)S(1)}, s32[2,5,5]{2,0,1:T(2,128)}, u32[]{:S(2)}) copy-start(s32[2,5,5]{2,0,1:T(2,128)} %param.14) | copy-start | bytes 604
  6.5 5.4 %copy-start = (bf16[2,640,640]{2,1,0:T(8,128)(2,1)S(1)}, bf16[2,640,640]{2,1,0:T(8,128)(2,1)}, u32[]{:S(2)}) copy-start(bf16[2,640,640]{2,1,0:T(8,128)(2,1)} %param.9) | copy-start | bytes 4915204
  6.5 47.1 %all-gather.2.cloned.1.call-start = ((), (), s32[]{:S(2)}) async-start(), calls=%async_computation | async-start | bytes 2228224 | tf_op jit(solution)/shard_map/all_gather | solution.py:33
  8.9 5.3 %copy-start.3 = (s32[1,5]{1,0:T(1,128)S(1)}, s32[1,5]{1,0:T(1,128)}, u32[]{:S(2)}) copy-start(s32[1,5]{1,0:T(1,128)} %param.13) | copy-start | bytes 64
  18.5 54.4 %copy-start.1 = (bf16[2,640,640]{1,2,0:T(8,128)(2,1)}, bf16[2,640,640]{1,2,0:T(8,128)(2,1)S(1)}, u32[]{:S(2)}) copy-start(bf16[2,640,640]{1,2,0:T(8,128)(2,1)S(1)} %fusion.8) | copy-start | bytes 4915204
  68.5 4.4 %copy-start.2 = (bf16[640,640,1]{1,0,2:T(8,128)(2,1)S(1)}, bf16[640,640,1]{1,0,2:T(8,128)(2,1)}, u32[]{:S(2)}) copy-start(bf16[640,640,1]{1,0,2:T(8,128)(2,1)} %reshape.192) | copy-start | bytes 2457604
  97.9 4.5 %copy-start.5 = (s32[2]{0:T(128)S(1)}, s32[2]{0:T(128)}, u32[]{:S(2)}) copy-start(s32[2]{0:T(128)} %param.15) | copy-start | bytes 28
  99.4 56.5 %collective-permute-start.1 = (bf16[640,640]{0,1:T(8,128)(2,1)S(1)}, bf16[640,640]{0,1:T(8,128)(2,1)S(1)}, u32[]{:S(2)}, u32[]{:S(2)}) collective-permute-start(bf16[640,640]{0,1:T(8,128)(2,1)S(1)} %get-tuple-element.6), channel_id=1, source_target_pairs={{0,8},{1,9},{2,10},{3,11},{4,12},{5,13},{6,14},{7,15},{8,0},{9,1},... | collective-permute-start | bytes 2457608 | tf_op jit(solution)/shard_map/ppermute | solution.py:16
  100.2 73.3 %collective-permute-start = (bf16[640,640]{0,1:T(8,128)(2,1)S(1)}, bf16[640,640]{0,1:T(8,128)(2,1)S(1)}, u32[]{:S(2)}, u32[]{:S(2)}) collective-permute-start(bf16[640,640]{0,1:T(8,128)(2,1)S(1)} %get-tuple-element.5), channel_id=1, source_target_pairs={{0,8},{1,9},{2,10},{3,11},{4,12},{5,13},{6,14},{7,15},{8,0},{9,1},... | collective-permute-start | bytes 2457608 | tf_op jit(solution)/shard_map/ppermute | solution.py:16
Sparse Core Ops, SparseCore 0:
  9.5 44.0 all-gather.1

commit v2 on v1

v2 whole, which is shorter than its diff:
```python
import functools

import jax
import jax.numpy as jnp
from jax import lax
from jax.experimental import pallas as pl
from jax.experimental.pallas import tpu as pltpu
from jax.sharding import PartitionSpec as P

VT = 128
KDOM = 5
OPS = 5
DOM = 640
NEED_DEV = 125
PB = 2
PLANE = 4
STRIPS = PB * KDOM
MESH = pl.DeviceIdType.MESH


def kernel(
    n, depth,
    ids, slots, extent, flags, amps_hbm, ints_hbm, stored, out,
    tiles, ops, amps, ints, masked, local, outgoing, incoming, final,
    own_sem, load_sem, z_send, z_recv, y_send, y_recv, c_send, c_recv,
    strip_send, strip_recv, out_sem,
):
    planes = n // PLANE
    me = lax.axis_index("pair")
    plane, place = me // PLANE, me % PLANE
    across = (place + 2) % PLANE
    twin = place // 2 * 2 + (1 - place % 2)
    y_mate, c_mate = plane * PLANE + across, plane * PLANE + twin
    mirror = lax.rem(me + n // 2, n)

    def plane_at(step):
        return lax.rem(plane + step + planes, planes)

    def block(index):
        return tiles.at[pl.ds(index * depth, depth)]

    def remote(source, target, send_sem, recv_sem, device):
        return pltpu.make_async_remote_copy(
            src_ref=source, dst_ref=target, send_sem=send_sem, recv_sem=recv_sem,
            device_id={"pair": device}, device_id_type=MESH,
        )

    loads = [
        pltpu.make_async_copy(amps_hbm, amps, load_sem.at[0]),
        pltpu.make_async_copy(ints_hbm, ints, load_sem.at[1]),
        pltpu.make_async_copy(stored, block(me), own_sem),
    ]
    for load in loads:
        load.start()

    barrier = pltpu.get_barrier_semaphore()
    for step in range(1, planes):
        pl.semaphore_signal(
            barrier, inc=1, device_id={"pair": plane_at(step) * PLANE + place},
            device_id_type=MESH,
        )
    for mate in (y_mate, c_mate):
        pl.semaphore_signal(barrier, inc=1, device_id={"pair": mate}, device_id_type=MESH)
    pl.semaphore_wait(barrier, planes + 1)

    sends = []

    def go(copy):
        copy.start()
        sends.append(copy)

    for step in range(1, planes):
        go(remote(stored, block(me), z_send.at[step], z_recv.at[step],
                  plane_at(step) * PLANE + place))
    go(remote(stored, block(me), y_send.at[0], y_recv.at[0], y_mate))
    go(remote(stored, block(me), c_send.at[0, 0], c_recv.at[0, 0], c_mate))

    def slot_sent(t):
        return jnp.where(slots[0] == t, 0, 1)

    rows_of = lax.broadcasted_iota(jnp.int32, (VT, VT), 0)
    columns_of = lax.broadcasted_iota(jnp.int32, (VT, VT), 1)

    def live(q, a, b):
        inside = (rows_of < extent[0, a]) & (columns_of < extent[0, b])
        return jnp.where(inside, flags[q, a, b].astype(jnp.float32), 0.0)

    def strip_rows(a):
        return pl.ds(pl.multiple_of(a * VT, VT), VT)

    loads[0].wait()

    def mask_strip(i, carry):
        t, a = i // KDOM, i % KDOM
        q = slot_sent(t)
        for b in range(KDOM):
            cols = slice(b * VT, (b + 1) * VT)
            value = amps[q, strip_rows(a), cols].astype(jnp.float32)
            masked[t, strip_rows(a), cols] = (value * live(q, a, b)).astype(jnp.bfloat16)
        return carry

    lax.fori_loop(0, STRIPS, mask_strip, 0)
    loads[1].wait()
    loads[2].wait()

    def forward_y(step):
        index = plane_at(-step) * PLANE + across
        remote(block(index), block(index), y_send.at[step], y_recv.at[step], y_mate).wait_recv()
        go(remote(block(index), block(index), c_send.at[1, step], c_recv.at[1, step], c_mate))

    for step in range(1, planes):
        index = plane_at(-step) * PLANE + place
        remote(block(index), block(index), z_send.at[step], z_recv.at[step], c_mate).wait_recv()
        go(remote(block(index), block(index), y_send.at[step], y_recv.at[step], y_mate))
        go(remote(block(index), block(index), c_send.at[0, step], c_recv.at[0, step], c_mate))
        forward_y(step - 1)
    forward_y(planes - 1)
    for step in range(planes):
        for half, origin in enumerate((twin, (twin + 2) % PLANE)):
            index = plane_at(-step) * PLANE + origin
            remote(block(index), block(index), c_send.at[half, step], c_recv.at[half, step],
                   c_mate).wait_recv()

    def place_tiles(i, carry):
        o, a = i // KDOM, i % KDOM
        for c in range(KDOM):
            ops[a, o, :, c * VT:(c + 1) * VT] = tiles[ids[0, i * KDOM + c]]
        return carry

    lax.fori_loop(0, OPS * KDOM, place_tiles, 0)

    def send_strip(i):
        return remote(outgoing.at[i], incoming.at[i], strip_send.at[i], strip_recv.at[i], mirror)

    def compute_strip(i, carry):
        t, a = i // KDOM, i % KDOM
        q = slot_sent(t)
        first = jnp.dot(
            ops[a].reshape(OPS * VT, DOM), masked[t], preferred_element_type=jnp.float32
        )
        total = ints[q, strip_rows(a), :].astype(jnp.float32) + first[:VT]
        for o in range(OPS):
            if o == 0:
                left = masked[t, strip_rows(a), :]
            else:
                left = first[o * VT:(o + 1) * VT].astype(jnp.bfloat16)
            total += lax.dot_general(
                left, ops[:, o].reshape(DOM, DOM), (((1,), (1,)), ((), ())),
                preferred_element_type=jnp.float32,
            )
        local[t, strip_rows(a), :] = total
        outgoing[i] = total.T.astype(jnp.bfloat16)
        send_strip(i).start()
        return carry

    lax.fori_loop(0, STRIPS, compute_strip, 0)

    def write_strip(i):
        return pltpu.make_async_copy(
            final.at[i], out.at[i // KDOM, :, strip_rows(i % KDOM)], out_sem.at[i]
        )

    def finish_strip(i, carry):
        q, b = i // KDOM, i % KDOM
        send_strip(i).wait_recv()
        mine = slots[q]
        for a in range(KDOM):
            rows = slice(a * VT, (a + 1) * VT)
            both = local[mine, rows, strip_rows(b)] + incoming[i, rows, :].astype(jnp.float32)
            final[i, rows, :] = both * live(q, a, b)
        write_strip(i).start()
        return carry

    lax.fori_loop(0, STRIPS, finish_strip, 0)

    def drain(i, carry):
        send_strip(i).wait_send()
        write_strip(i).wait()
        return carry

    lax.fori_loop(0, STRIPS, drain, 0)
    for copy in sends:
        copy.wait_send()


def shards(
    amplitudes, pair_ints, int_tiles, tile_owner, tile_slot, tile_extent, tile_mask, mirror_slot
):
    n = lax.axis_size("pair")
    depth = int_tiles.shape[0]
    planes = n // PLANE
    first = lax.axis_index("pair") * NEED_DEV
    owners = lax.dynamic_slice(tile_owner, (first, 0), (NEED_DEV, 1)).reshape(1, NEED_DEV)
    places = lax.dynamic_slice(tile_slot, (first,), (NEED_DEV,)).reshape(1, NEED_DEV)
    ids = owners * depth + places
    bf16, f32 = jnp.bfloat16, jnp.float32
    dma = pltpu.SemaphoreType.DMA
    smem, anywhere = pl.BlockSpec(memory_space=pltpu.SMEM), pl.BlockSpec(memory_space=pl.ANY)
    return pl.pallas_call(
        functools.partial(kernel, n, depth),
        out_shape=jax.ShapeDtypeStruct((PB, DOM, DOM), f32),
        in_specs=[smem] * 4 + [anywhere] * 3,
        out_specs=anywhere,
        scratch_shapes=[
            pltpu.VMEM((n * depth, VT, VT), bf16),
            pltpu.VMEM((KDOM, OPS, VT, DOM), bf16),
            pltpu.VMEM((PB, DOM, DOM), bf16),
            pltpu.VMEM((PB, DOM, DOM), bf16),
            pltpu.VMEM((PB, DOM, DOM), bf16),
            pltpu.VMEM((PB, DOM, DOM), f32),
            pltpu.VMEM((STRIPS, DOM, VT), bf16),
            pltpu.VMEM((STRIPS, DOM, VT), bf16),
            pltpu.VMEM((STRIPS, DOM, VT), f32),
            dma, dma((2,)),
            dma((planes,)), dma((planes,)), dma((planes,)), dma((planes,)),
            dma((2, planes)), dma((2, planes)),
            dma((STRIPS,)), dma((STRIPS,)), dma((STRIPS,)),
        ],
        compiler_params=pltpu.CompilerParams(
            collective_id=0, has_side_effects=True, vmem_limit_bytes=56 * 1024 * 1024
        ),
        cost_estimate=pl.CostEstimate(
            flops=20 * PB * DOM**3, bytes_accessed=7 * 1024 * 1024, transcendentals=0
        ),
    )(ids, mirror_slot, tile_extent, tile_mask, amplitudes, pair_ints, int_tiles)


def solution(mesh):
    in_specs = (
        P(("frag", "pair"), None, None),
        P(("frag", "pair"), None, None),
        P(("frag", "pair"), None, None),
        P("frag", None),
        P("frag"),
        P(("frag", "pair"), None),
        P(("frag", "pair"), None, None),
        P(("frag", "pair")),
    )
    out_specs = P(("frag", "pair"), None, None)
    return jax.shard_map(shards, mesh=mesh, in_specs=in_specs, out_specs=out_specs, check_vma=False)
```

time: 190 us -> 108 us (0.57)
  waiting for transfers between devices: 107 us -> 0 us
  Pallas kernels: 0 us -> 102 us
  local copies, waits for them, and re-layouts: 30.6 us -> 5.13 us
  matrix products: 22.4 us -> 0 us
  between operations: 13.6 us -> 0.01 us
  other arithmetic: 13.4 us -> 1.29 us
  starting transfers between devices: 2.99 us -> 0 us
    pallas_call x0 -> x1, Pallas kernels: none -> 102 us  [shards(): pl.pallas_call(functools.partial(kernel, n, depth), out_shape=jax.ShapeDt...]
    ppermute x2 -> x0, waiting for transfers between devices: 71 us -> none  [passed_along(): return lax.ppermute(value, axis, pairs)]
    all_gather x1 -> x0, waiting for transfers between devices: 35.1 us -> none  [shards(): stored = lax.all_gather(int_tiles, 'pair', axis=0, tiled=True)]
    dot_general x3 -> x0, matrix products: 22.4 us -> none  [the longest x1 14.7 us: shards(): jnp.einsum('qpad,pbd->qab', half_ladder, factors, preferred_element_type=...]
    slice x3 -> x0, local copies, waits for them, and re-layouts: 10.4 us -> none  [the longest x2 10.2 us: shards(): factors = operators[1:]]
    gather x3 -> x0, local copies, waits for them, and re-layouts: 7.18 us -> none  [the longest x1 4.58 us: shards(): op_tiles = jnp.take(stored, own_ids, axis=0)]
    transpose x1 -> x0, other arithmetic: 5.11 us -> none  [shards(): operators = op_tiles.reshape(1 + NAUXW, KDOM, KDOM, VT, VT).transpose(0,...]
    mul x3 -> x0, other arithmetic: 4.18 us -> none  [the longest x1 3.02 us: shards(): return dmask.astype(jnp.float32) * (local_res + mirror)]
  transfers between devices with their start and end apart: 3 -> 0, of which waited for: 3 -> 0; matrix products, arithmetic and copies ran while one was open for 6% -> 0% of each run, Pallas kernels for 0% -> 0%
where the time goes in v2:
time: 108 us
  Pallas kernels  102 us (94%)
  local copies, waits for them, and re-layouts  5.13 us (5%)
  other arithmetic  1.29 us (1%)
    pallas_call x1, Pallas kernels, shards(): pl.pallas_call(functools.partial(kernel, n, depth), out_shape=jax.ShapeDt...  102 us
    unnamed x2, local copies, waits for them, and re-layouts  5.13 us

profile of v2, /device:TPU:0, one launch (start us, length us, event | category | flops | bytes accessed | tf_op | source)
XLA Modules:
  0.0 108.2 jit_solution(17941231500212431123)
XLA Ops:
  0.0 1.3 %fusion.ids = s32[1,125]{1,0:T(1,128)} fusion(s32[2000]{0:T(1024)} %param.12, s32[]{:T(128)S(6)} %select_n.4, s32[2000,1]{0,1:T(1,128)} %param.11), kind=kLoop, calls=%fused_computation.1 | loop fusion | flops 250 | bytes 1504 | tf_op jit(solution)/shard_map/add | solution.py:195
  1.3 1.3 %copy.9.flags = s32[2,5,5]{2,1,0:T(8,128)} copy(s32[2,5,5]{2,0,1:T(2,128)} %param.14) | data formatting | bytes 400 | tf_op args[6]
  2.6 101.8 %shard_map.82 = f32[2,640,640]{2,1,0:T(8,128)} custom-call(s32[1,125]{1,0:T(1,128)} %fusion.ids, s32[2]{0:T(128)} %slots.1, s32[1,5]{1,0:T(1,128)} %extent.1, s32[2,5,5]{2,1,0:T(8,128)} %copy.9.flags, bf16[2,640,640]{2,1,0:T(8,128)(2,1)} %amps_hbm.1, bf16[2,640,640]{2,1,0:T(8,128)(2,1)} %ints_hbm.1, bf16[4,128,128]{2,1,0:T(8,128)(2,1)} %stored.1), custom_call_target="tpu_custom_call" | custom-call | flops 10485760000 | bytes 7340032 | tf_op jit(solution)/shard_map/pallas_call | solution.py:199
  104.3 3.8 %copy.11 = f32[2,640,640]{2,1,0:T(8,128)} copy(f32[2,640,640]{2,1,0:T(8,128)} %shard_map.82) | data formatting | bytes 6553600

commit v3 on v2

--- a/solution.py
+++ b/solution.py
@@ -20,7 +20,7 @@
 
 def kernel(
     n, depth,
-    ids, slots, extent, flags, amps_hbm, ints_hbm, stored, out,
+    table, slots, extent, amps_hbm, ints_hbm, stored, out,
     tiles, ops, amps, ints, masked, local, outgoing, incoming, final,
     own_sem, load_sem, z_send, z_recv, y_send, y_recv, c_send, c_recv,
     strip_send, strip_recv, out_sem,
@@ -36,8 +36,14 @@
     def plane_at(step):
         return lax.rem(plane + step + planes, planes)
 
-    def block(index):
-        return tiles.at[pl.ds(index * depth, depth)]
+    pieces = z_send.shape[2]
+    size = depth // pieces
+
+    def hop_plane(way, step):
+        return plane - step if way == 0 else plane + step
+
+    def block(index, piece):
+        return tiles.at[pl.ds(index * depth + piece * size, size)]
 
     def remote(source, target, send_sem, recv_sem, device):
         return pltpu.make_async_remote_copy(
@@ -48,7 +54,7 @@
     loads = [
         pltpu.make_async_copy(amps_hbm, amps, load_sem.at[0]),
         pltpu.make_async_copy(ints_hbm, ints, load_sem.at[1]),
-        pltpu.make_async_copy(stored, block(me), own_sem),
+        pltpu.make_async_copy(stored, tiles.at[pl.ds(me * depth, depth)], own_sem),
     ]
     for load in loads:
         load.start()
@@ -63,17 +69,44 @@
         pl.semaphore_signal(barrier, inc=1, device_id={"pair": mate}, device_id_type=MESH)
     pl.semaphore_wait(barrier, planes + 1)
 
-    sends = []
-
-    def go(copy):
-        copy.start()
-        sends.append(copy)
-
-    for step in range(1, planes):
-        go(remote(stored, block(me), z_send.at[step], z_recv.at[step],
-                  plane_at(step) * PLANE + place))
-    go(remote(stored, block(me), y_send.at[0], y_recv.at[0], y_mate))
-    go(remote(stored, block(me), c_send.at[0, 0], c_recv.at[0, 0], c_mate))
+    def over_z(way, step, piece, origin):
+        target = plane + 1 if way == 0 else plane - 1
+        return remote(
+            origin, block(hop_plane(way, step) * PLANE + place, piece),
+            z_send.at[way, step, piece], z_recv.at[way, step, piece], target * PLANE + place,
+        )
+
+    def over_y(way, step, piece, origin):
+        return remote(
+            origin, block(hop_plane(way, step) * PLANE + place, piece),
+            y_send.at[way, step, piece], y_recv.at[way, step, piece], y_mate,
+        )
+
+    def over_c(half, way, step, piece, origin):
+        source = place if half == 0 else across
+        return remote(
+            origin, block(hop_plane(way, step) * PLANE + source, piece),
+            c_send.at[half, way, step, piece], c_recv.at[half, way, step, piece], c_mate,
+        )
+
+    def arrived(index, piece, sem):
+        held = block(index, piece)
+        remote(held, held, c_send.at[0, 0, 0, piece], sem, c_mate).wait_recv()
+
+    def can_go_on(way):
+        return plane < planes - 1 if way == 0 else plane > 0
+
+    def comes(way, step):
+        return plane >= step if way == 0 else plane + step < planes
+
+    every = [(way, step) for step in range(planes) for way in range(2) if step or not way]
+
+    for piece in range(pieces):
+        own = stored.at[pl.ds(piece * size, size)]
+        for way in range(2):
+            pl.when(can_go_on(way))(lambda: over_z(way, 0, piece, own).start())
+        over_y(0, 0, piece, own).start()
+        over_c(0, 0, 0, piece, own).start()
 
     def slot_sent(t):
         return jnp.where(slots[0] == t, 0, 1)
@@ -83,7 +116,7 @@
 
     def live(q, a, b):
         inside = (rows_of < extent[0, a]) & (columns_of < extent[0, b])
-        return jnp.where(inside, flags[q, a, b].astype(jnp.float32), 0.0)
+        return jnp.where(inside, table[0, NEED_DEV + q * KDOM**2 + a * KDOM + b].astype(jnp.float32), 0.0)
 
     def strip_rows(a):
         return pl.ds(pl.multiple_of(a * VT, VT), VT)
@@ -103,28 +136,41 @@
     loads[1].wait()
     loads[2].wait()
 
-    def forward_y(step):
-        index = plane_at(-step) * PLANE + across
-        remote(block(index), block(index), y_send.at[step], y_recv.at[step], y_mate).wait_recv()
-        go(remote(block(index), block(index), c_send.at[1, step], c_recv.at[1, step], c_mate))
-
-    for step in range(1, planes):
-        index = plane_at(-step) * PLANE + place
-        remote(block(index), block(index), z_send.at[step], z_recv.at[step], c_mate).wait_recv()
-        go(remote(block(index), block(index), y_send.at[step], y_recv.at[step], y_mate))
-        go(remote(block(index), block(index), c_send.at[0, step], c_recv.at[0, step], c_mate))
-        forward_y(step - 1)
-    forward_y(planes - 1)
-    for step in range(planes):
+    def pass_z(way, step, piece):
+        index = hop_plane(way, step) * PLANE + place
+        held = block(index, piece)
+        arrived(index, piece, z_recv.at[way, step - 1, piece])
+        pl.when(can_go_on(way))(lambda: over_z(way, step, piece, held).start())
+        over_y(way, step, piece, held).start()
+        over_c(0, way, step, piece, held).start()
+
+    def pass_y(way, step, piece):
+        index = hop_plane(way, step) * PLANE + across
+        arrived(index, piece, y_recv.at[way, step, piece])
+        over_c(1, way, step, piece, block(index, piece)).start()
+
+    for step in range(1, planes + 1):
+        for piece in range(pieces):
+            for way in range(2):
+                if step < planes:
+                    pl.when(comes(way, step))(lambda: pass_z(way, step, piece))
+        for piece in range(pieces):
+            for way in range(2):
+                if (way, step - 1) in every:
+                    pl.when(comes(way, step - 1))(lambda: pass_y(way, step - 1, piece))
+
+    def pass_c(way, step, piece):
         for half, origin in enumerate((twin, (twin + 2) % PLANE)):
-            index = plane_at(-step) * PLANE + origin
-            remote(block(index), block(index), c_send.at[half, step], c_recv.at[half, step],
-                   c_mate).wait_recv()
+            arrived(hop_plane(way, step) * PLANE + origin, piece, c_recv.at[half, way, step, piece])
+
+    for way, step in every:
+        for piece in range(pieces):
+            pl.when(comes(way, step))(lambda: pass_c(way, step, piece))
 
     def place_tiles(i, carry):
         o, a = i // KDOM, i % KDOM
         for c in range(KDOM):
-            ops[a, o, :, c * VT:(c + 1) * VT] = tiles[ids[0, i * KDOM + c]]
+            ops[a, o, :, c * VT:(c + 1) * VT] = tiles[table[0, i * KDOM + c]]
         return carry
 
     lax.fori_loop(0, OPS * KDOM, place_tiles, 0)
@@ -179,8 +225,21 @@
         return carry
 
     lax.fori_loop(0, STRIPS, drain, 0)
-    for copy in sends:
-        copy.wait_send()
+    def sent(way, step, piece):
+        index = hop_plane(way, step) * PLANE + place
+        over_y(way, step, piece, block(index, piece)).wait_send()
+        for half in range(2):
+            over_c(half, way, step, piece, block(index, piece)).wait_send()
+
+    for way, step in every:
+        for piece in range(pieces):
+            pl.when(comes(way, step))(lambda: sent(way, step, piece))
+    for step in range(planes - 1):
+        for way in range(2):
+            for piece in range(pieces):
+                pl.when(comes(way, step) & can_go_on(way))(
+                    lambda: over_z(way, step, piece, block(me, piece)).wait_send()
+                )
 
 
 def shards(
@@ -189,17 +248,19 @@
     n = lax.axis_size("pair")
     depth = int_tiles.shape[0]
     planes = n // PLANE
+    pieces = 2 if depth % 2 == 0 else 1
     first = lax.axis_index("pair") * NEED_DEV
     owners = lax.dynamic_slice(tile_owner, (first, 0), (NEED_DEV, 1)).reshape(1, NEED_DEV)
     places = lax.dynamic_slice(tile_slot, (first,), (NEED_DEV,)).reshape(1, NEED_DEV)
     ids = owners * depth + places
+    table = jnp.concatenate([ids, tile_mask.reshape(1, PB * KDOM**2)], axis=1)
     bf16, f32 = jnp.bfloat16, jnp.float32
     dma = pltpu.SemaphoreType.DMA
     smem, anywhere = pl.BlockSpec(memory_space=pltpu.SMEM), pl.BlockSpec(memory_space=pl.ANY)
     return pl.pallas_call(
         functools.partial(kernel, n, depth),
         out_shape=jax.ShapeDtypeStruct((PB, DOM, DOM), f32),
-        in_specs=[smem] * 4 + [anywhere] * 3,
+        in_specs=[smem] * 3 + [anywhere] * 3,
         out_specs=anywhere,
         scratch_shapes=[
             pltpu.VMEM((n * depth, VT, VT), bf16),
@@ -212,8 +273,9 @@
             pltpu.VMEM((STRIPS, DOM, VT), bf16),
             pltpu.VMEM((STRIPS, DOM, VT), f32),
             dma, dma((2,)),
-            dma((planes,)), dma((planes,)), dma((planes,)), dma((planes,)),
-            dma((2, planes)), dma((2, planes)),
+            dma((2, planes, pieces)), dma((2, planes, pieces)),
+            dma((2, planes, pieces)), dma((2, planes, pieces)),
+            dma((2, 2, planes, pieces)), dma((2, 2, planes, pieces)),
             dma((STRIPS,)), dma((STRIPS,)), dma((STRIPS,)),
         ],
         compiler_params=pltpu.CompilerParams(
@@ -222,7 +284,7 @@
         cost_estimate=pl.CostEstimate(
             flops=20 * PB * DOM**3, bytes_accessed=7 * 1024 * 1024, transcendentals=0
         ),
-    )(ids, mirror_slot, tile_extent, tile_mask, amplitudes, pair_ints, int_tiles)
+    )(table, mirror_slot, tile_extent, amplitudes, pair_ints, int_tiles)
 
 
 def solution(mesh):

time: 108 us -> 103 us (0.954)
  Pallas kernels: 102 us -> 96.8 us
    pallas_call x1, Pallas kernels: 102 us -> 96.8 us  [shards(): pl.pallas_call(functools.partial(kernel, n, depth), out_shape=jax.ShapeDt...]
where the time goes in v3:
time: 103 us
  Pallas kernels  96.8 us (94%)
  local copies, waits for them, and re-layouts  4.62 us (4%)
  other arithmetic  1.42 us (1%)
    pallas_call x1, Pallas kernels, shards(): pl.pallas_call(functools.partial(kernel, n, depth), out_shape=jax.ShapeDt...  96.8 us
    unnamed x2, local copies, waits for them, and re-layouts  4.54 us

profile of v3, /device:TPU:0, one launch (start us, length us, event | category | flops | bytes accessed | tf_op | source)
XLA Modules:
  0.0 102.9 jit_solution(8159059501436812033)
XLA Ops:
  0.0 0.8 fusion
  0.8 0.7 copy.10
  1.5 0.1 reshape.10
  1.5 0.6 pad_add_fusion.table
  2.2 96.8 %shard_map.82 = f32[2,640,640]{2,1,0:T(8,128)} custom-call(s32[1,175]{1,0:T(1,128)} %pad_add_fusion.table, s32[2]{0:T(128)} %slots.1, s32[1,5]{1,0:T(1,128)} %extent.1, bf16[2,640,640]{2,1,0:T(8,128)(2,1)} %amps_hbm.1, bf16[2,640,640]{2,1,0:T(8,128)(2,1)} %ints_hbm.1, bf16[4,128,128]{2,1,0:T(8,128)(2,1)} %stored.1), custom_call_target="tpu_custom_call" | custom-call | flops 10485760000 | bytes 7340032 | tf_op jit(solution)/shard_map/pallas_call | solution.py:260
  99.0 3.8 %copy.12 = f32[2,640,640]{2,1,0:T(8,128)} copy(f32[2,640,640]{2,1,0:T(8,128)} %shard_map.82) | data formatting | bytes 6553600

commit v4 on v3

--- a/solution.py
+++ b/solution.py
@@ -20,7 +20,7 @@
 
 def kernel(
     n, depth,
-    table, slots, extent, amps_hbm, ints_hbm, stored, out,
+    owners, places, slots, extent, flags, amps_hbm, ints_hbm, stored, out,
     tiles, ops, amps, ints, masked, local, outgoing, incoming, final,
     own_sem, load_sem, z_send, z_recv, y_send, y_recv, c_send, c_recv,
     strip_send, strip_recv, out_sem,
@@ -116,7 +116,7 @@
 
     def live(q, a, b):
         inside = (rows_of < extent[0, a]) & (columns_of < extent[0, b])
-        return jnp.where(inside, table[0, NEED_DEV + q * KDOM**2 + a * KDOM + b].astype(jnp.float32), 0.0)
+        return jnp.where(inside, flags[a, q, b].astype(jnp.float32), 0.0)
 
     def strip_rows(a):
         return pl.ds(pl.multiple_of(a * VT, VT), VT)
@@ -167,10 +167,14 @@
         for piece in range(pieces):
             pl.when(comes(way, step))(lambda: pass_c(way, step, piece))
 
+    def tile_at(index):
+        row = me * NEED_DEV + index
+        return owners[0, row] * depth + places[row]
+
     def place_tiles(i, carry):
         o, a = i // KDOM, i % KDOM
         for c in range(KDOM):
-            ops[a, o, :, c * VT:(c + 1) * VT] = tiles[table[0, i * KDOM + c]]
+            ops[a, o, :, c * VT:(c + 1) * VT] = tiles[tile_at(i * KDOM + c)]
         return carry
 
     lax.fori_loop(0, OPS * KDOM, place_tiles, 0)
@@ -249,18 +253,13 @@
     depth = int_tiles.shape[0]
     planes = n // PLANE
     pieces = 2 if depth % 2 == 0 else 1
-    first = lax.axis_index("pair") * NEED_DEV
-    owners = lax.dynamic_slice(tile_owner, (first, 0), (NEED_DEV, 1)).reshape(1, NEED_DEV)
-    places = lax.dynamic_slice(tile_slot, (first,), (NEED_DEV,)).reshape(1, NEED_DEV)
-    ids = owners * depth + places
-    table = jnp.concatenate([ids, tile_mask.reshape(1, PB * KDOM**2)], axis=1)
     bf16, f32 = jnp.bfloat16, jnp.float32
     dma = pltpu.SemaphoreType.DMA
     smem, anywhere = pl.BlockSpec(memory_space=pltpu.SMEM), pl.BlockSpec(memory_space=pl.ANY)
     return pl.pallas_call(
         functools.partial(kernel, n, depth),
         out_shape=jax.ShapeDtypeStruct((PB, DOM, DOM), f32),
-        in_specs=[smem] * 3 + [anywhere] * 3,
+        in_specs=[smem] * 5 + [anywhere] * 3,
         out_specs=anywhere,
         scratch_shapes=[
             pltpu.VMEM((n * depth, VT, VT), bf16),
@@ -279,12 +278,18 @@
             dma((STRIPS,)), dma((STRIPS,)), dma((STRIPS,)),
         ],
         compiler_params=pltpu.CompilerParams(
-            collective_id=0, has_side_effects=True, vmem_limit_bytes=56 * 1024 * 1024
+            collective_id=0, has_side_effects=True, vmem_limit_bytes=(30 + n * depth // 32) * 1024 * 1024
         ),
         cost_estimate=pl.CostEstimate(
             flops=20 * PB * DOM**3, bytes_accessed=7 * 1024 * 1024, transcendentals=0
         ),
-    )(table, mirror_slot, tile_extent, amplitudes, pair_ints, int_tiles)
+    )(*(
+        pltpu.with_memory_space_constraint(value, pltpu.HBM)
+        for value in (
+            tile_owner.T, tile_slot, mirror_slot, tile_extent,
+            jnp.transpose(tile_mask, (1, 0, 2)), amplitudes, pair_ints, int_tiles,
+        )
+    ))
 
 
 def solution(mesh):

time: 103 us -> 98.6 us (0.957)
  local copies, waits for them, and re-layouts: 4.62 us -> 1.71 us
  other arithmetic: 1.42 us -> 0 us
    unnamed x2 -> x1, local copies, waits for them, and re-layouts: 4.54 us -> 1.71 us
where the time goes in v4:
time: 98.6 us; the launch traced here: 98.4 us
  Pallas kernels  96.7 us (98%)
  local copies, waits for them, and re-layouts  1.71 us (2%)
    pallas_call x1, Pallas kernels, shards(): pl.pallas_call(functools.partial(kernel, n, depth), out_shape=jax.ShapeDt...  96.7 us

profile of v4, /device:TPU:0, one launch (start us, length us, event | category | flops | bytes accessed | tf_op | source)
XLA Modules:
  0.0 98.4 jit_solution(15962157407513503033)
XLA Ops:
  0.0 96.7 %shard_map.82 = f32[2,640,640]{2,1,0:T(8,128)S(1)} custom-call(s32[1,2000]{1,0:T(1,128)} %bitcast.2, s32[2000]{0:T(1024)} %places.1, s32[2]{0:T(128)} %slots.1, s32[1,5]{1,0:T(1,128)} %extent.1, s32[5,2,5]{2,1,0:T(2,128)} %bitcast.3, bf16[2,640,640]{2,1,0:T(8,128)(2,1)} %amps_hbm.1, bf16[2,640,640]{2,1,0:T(8,128)(2,1)} %ints_hbm.1, bf16[4,128,128]{2,1,0:T(8,128)(2,1)} %stored.1), custom_call_target="tpu_custom_call" | custom-call | flops 10485760000 | bytes 7340032 | tf_op jit(solution)/shard_map/pallas_call | solution.py:259
  96.7 1.7 %copy.10 = f32[2,640,640]{2,1,0:T(8,128)} copy(f32[2,640,640]{2,1,0:T(8,128)S(1)} %shard_map.82) | data formatting | bytes 6553600
